TPU v7x, 32 devices: a whole 2x2x4 slice. The times are simulated.
32 devices in a mesh: dp: 8 (over z, y), ctx: 2 (over x), fsdp: 2 (over core).
Axes of the slice: x: 2, y: 2, z: 4, core: 2. Of those that a mesh axis runs over, the one named last changes fastest.
Arguments:
- layer_input: bfloat16 [16, 1024, 896], P(('dp', 'fsdp'), 'ctx'), may hold values from -6 to 6
- w_qkv: bfloat16 [896, 1152], P('fsdp'), may hold values from -0.1875 to 0.1875
- b_qkv: bfloat16 [1152], P('fsdp'), may hold values from -3 to 3
- g_attn: bfloat16 [896], P('fsdp'), may hold values from 0.25 to 1.75
- w_out: bfloat16 [896, 896], P('fsdp'), may hold values from -0.75 to 0.75
- g_mlp: bfloat16 [896], P('fsdp'), may hold values from 0.25 to 1.75
- w_gate: bfloat16 [896, 4864], P('fsdp'), may hold values from -0.1875 to 0.1875
- w_up: bfloat16 [896, 4864], P('fsdp'), may hold values from -0.1875 to 0.1875
- w_down: bfloat16 [4864, 896], P('fsdp'), may hold values from -0.078125 to 0.078125
- cotangent: bfloat16 [16, 1024, 896], P(('dp', 'fsdp'), 'ctx'), may hold values from -6 to 6
Outputs:
- activations: float32 [16, 1024, 896], P(('dp', 'fsdp'), 'ctx')
- grad_input: float32 [16, 1024, 896], P(('dp', 'fsdp'), 'ctx')
- grad_w_qkv: float32 [896, 1152], P('fsdp', ('dp', 'ctx'))
- grad_b_qkv: float32 [1152], P('fsdp')
- grad_g_attn: float32 [896], P('fsdp')
- grad_w_out: float32 [896, 896], P('fsdp', ('dp', 'ctx'))
- grad_g_mlp: float32 [896], P('fsdp')
- grad_w_gate: float32 [896, 4864], P('fsdp', ('dp', 'ctx'))
- grad_w_up: float32 [896, 4864], P('fsdp', ('dp', 'ctx'))
- grad_w_down: float32 [4864, 896], P('fsdp', ('dp', 'ctx'))
All inputs are finite; a program needn't handle non-finite values.
Results may differ from a plain program's by a relative error of at most 0.015.
Values may be sent and summed in bfloat16 or wider, within the bound.
A program may use at most 192 MiB of HBM per device.

v0:
```python
import jax
import jax.numpy as jnp
from jax import lax
from jax.sharding import PartitionSpec as P

HQ = 14
KVH = 2
HD = 64
ATT = 896
QKV = 1152
GROUP = 7


epsilon = 1e-06
rope_base = 1000000.0
masked_score = -1e30
highest = lax.Precision.HIGHEST


def shifted(block, axis, distance):
    devices = range(lax.axis_size(axis))
    route = [(i - distance, i) for i in devices if i - distance in devices]
    return lax.ppermute(block, axis, route)


def shifted_2(value, axis, steps):
    count = lax.axis_size(axis)
    pairs = [(source, (source + steps) % count) for source in range(count)]
    return lax.ppermute(value, axis, pairs)


def tables(positions):
    frequency = rope_base ** (-(2.0 * jnp.arange(HD // 2, dtype=jnp.float32)) / HD)
    angles = positions[:, None] * frequency[None, :]
    cos_table = jnp.cos(angles)
    sin_table = jnp.sin(angles)
    return (
        jnp.concatenate([cos_table, cos_table], -1),
        jnp.concatenate([sin_table, sin_table], -1),
    )


def rotate(heads_in, cos_table, sin_table):
    half_dim = HD // 2
    turned = jnp.concatenate([-heads_in[..., half_dim:], heads_in[..., :half_dim]], -1)
    return heads_in * cos_table[:, None, :] + turned * sin_table[:, None, :]


def unrotate(grads_in, cos_table, sin_table):
    half_dim = HD // 2
    scaled = grads_in * sin_table[:, None, :]
    turned = jnp.concatenate([scaled[..., half_dim:], -scaled[..., :half_dim]], -1)
    return grads_in * cos_table[:, None, :] + turned


def contract_rows(left, right):
    return lax.dot_general(
        left, right, (((0,), (0,)), ((), ())), preferred_element_type=jnp.float32
    )


def times_transpose(left, right):
    return lax.dot_general(
        left, right, (((1,), (1,)), ((), ())), preferred_element_type=jnp.float32
    )


def move_block(key_block):
    return shifted(key_block, "ctx", 1)


def move_grads(grad_pair):
    return shifted_2(grad_pair.astype(jnp.bfloat16), "ctx", 1).astype(grad_pair.dtype)


def per_device(layer_input, w_qkv, b_qkv, g_attn, w_out, g_mlp, w_gate, w_up, w_down, cotangent):
    sequences, local_len, model_width = layer_input.shape
    token_rows = sequences * local_len
    key_width = KVH * HD
    query_rows = local_len * GROUP
    cycle_size = lax.axis_size("ctx")
    own_index = lax.axis_index("ctx")
    gathered = (
        lax.all_gather(w_qkv, "fsdp", axis=0, tiled=True),
        lax.all_gather(b_qkv, "fsdp", axis=0, tiled=True),
        lax.all_gather(g_attn, "fsdp", axis=0, tiled=True),
        lax.all_gather(w_out, "fsdp", axis=0, tiled=True),
        lax.all_gather(g_mlp, "fsdp", axis=0, tiled=True),
        lax.all_gather(w_gate, "fsdp", axis=0, tiled=True),
        lax.all_gather(w_up, "fsdp", axis=0, tiled=True),
        lax.all_gather(w_down, "fsdp", axis=0, tiled=True),
    )
    full_qkv, full_bias, gain_attn, full_out, gain_mlp, full_gate, full_up, full_down = gathered
    gain_one = gain_attn.astype(jnp.float32)
    gain_two = gain_mlp.astype(jnp.float32)
    inputs = layer_input.reshape(token_rows, model_width).astype(jnp.float32)
    scale_one = lax.rsqrt(jnp.mean(inputs * inputs, axis=-1, keepdims=True) + epsilon)
    normed_one = (inputs * scale_one * gain_one).astype(jnp.bfloat16)
    joined = jnp.dot(normed_one, full_qkv, preferred_element_type=jnp.float32) + full_bias.astype(
        jnp.float32
    )
    positions = (own_index * local_len + jnp.arange(local_len, dtype=jnp.int32)).astype(jnp.float32)
    cos_table, sin_table = tables(positions)
    head_shape = (sequences, KVH, query_rows, HD)

    def to_rows(grouped):
        return (
            grouped.reshape(sequences, KVH, local_len, GROUP, HD)
            .transpose(0, 2, 1, 3, 4)
            .reshape(token_rows, ATT)
        )

    def to_groups(flat):
        return (
            flat.reshape(sequences, local_len, KVH, GROUP, HD)
            .transpose(0, 2, 1, 3, 4)
            .reshape(head_shape)
        )

    query_heads = rotate(
        joined[:, :ATT].reshape(sequences, local_len, HQ, HD), cos_table, sin_table
    )
    queries = to_groups(query_heads.astype(jnp.bfloat16).reshape(token_rows, ATT))
    rotated_keys = rotate(
        joined[:, ATT : ATT + key_width].reshape(sequences, local_len, KVH, HD),
        cos_table,
        sin_table,
    )
    values = joined[:, ATT + key_width :].astype(jnp.bfloat16)
    own_block = jnp.stack(
        [
            rotated_keys.astype(jnp.bfloat16).reshape(sequences, local_len, key_width),
            values.reshape(sequences, local_len, key_width),
        ]
    )
    score_scale = HD ** (-0.5)
    query_token = own_index * local_len + jnp.arange(query_rows, dtype=jnp.int32) // GROUP

    def scores_for(key_block, source):
        key_heads = key_block[0].reshape(sequences, local_len, KVH, HD)
        logits = (
            jnp.einsum("sgrd,sugd->sgru", queries, key_heads, preferred_element_type=jnp.float32)
            * score_scale
        )
        key_token = source * local_len + jnp.arange(local_len, dtype=jnp.int32)
        return (logits, key_token[None, :] <= query_token[:, None])

    def visit_all(running, visitor):

        def advance(turn_index, packed):
            state_in, key_block = packed
            source = (own_index - turn_index) % cycle_size
            state_in = lax.cond(
                source <= own_index, lambda: visitor(state_in, key_block, source), lambda: state_in
            )
            return (state_in, move_block(key_block))

        running, key_block = lax.fori_loop(0, cycle_size - 1, advance, (running, own_block))
        source = (own_index + 1) % cycle_size
        return lax.cond(
            source <= own_index, lambda: visitor(running, key_block, source), lambda: running
        )

    def extreme(running, key_block, source):
        row_top, row_total = running
        logits, visible = scores_for(key_block, source)
        logits = jnp.where(visible, logits, masked_score)
        new_top = jnp.maximum(row_top, jnp.max(logits, axis=-1))
        row_total = row_total * jnp.exp(row_top - new_top) + jnp.sum(
            jnp.exp(logits - new_top[..., None]), axis=-1
        )
        return (new_top, row_total)

    row_shape = (sequences, KVH, query_rows)
    row_top, row_total = visit_all(
        (jnp.full(row_shape, masked_score, jnp.float32), jnp.zeros(row_shape, jnp.float32)), extreme
    )
    log_total = row_top + jnp.log(row_total)

    def probabilities(key_block, source):
        logits, visible = scores_for(key_block, source)
        return jnp.where(visible, jnp.exp(logits - log_total[..., None]), 0.0)

    def accumulate(running, key_block, source):
        mixed_low, mixed_exact = running
        weights_prob = probabilities(key_block, source)
        value_heads = key_block[1].reshape(sequences, local_len, KVH, HD)
        mixed_low = mixed_low + jnp.einsum(
            "sgru,sugd->sgrd",
            weights_prob.astype(jnp.bfloat16),
            value_heads,
            preferred_element_type=jnp.float32,
        )
        mixed_exact = mixed_exact + jnp.einsum(
            "sgru,sugd->sgrd",
            weights_prob,
            value_heads.astype(jnp.float32),
            precision=highest,
            preferred_element_type=jnp.float32,
        )
        return (mixed_low, mixed_exact)

    zero_heads = jnp.zeros(head_shape, jnp.float32)
    mixed_low, mixed_exact = visit_all((zero_heads, zero_heads), accumulate)
    attended = to_rows(mixed_low).astype(jnp.bfloat16)
    hidden = inputs + jnp.dot(attended, full_out, preferred_element_type=jnp.float32)
    scale_two = lax.rsqrt(jnp.mean(hidden * hidden, axis=-1, keepdims=True) + epsilon)
    normed_two = (hidden * scale_two * gain_two).astype(jnp.bfloat16)
    gate_pre = jnp.dot(normed_two, full_gate, preferred_element_type=jnp.float32)
    up_value = jnp.dot(normed_two, full_up, preferred_element_type=jnp.float32)
    swish = jax.nn.silu(gate_pre)
    product = (swish * up_value).astype(jnp.bfloat16)
    activations = hidden + jnp.dot(product, full_down, preferred_element_type=jnp.float32)
    upstream = cotangent.reshape(token_rows, model_width)
    grad_down = contract_rows(product, upstream)
    grad_product = times_transpose(upstream, full_down)
    gate_sig = jax.nn.sigmoid(gate_pre)
    grad_gate = (grad_product * up_value * gate_sig * (1.0 + gate_pre * (1.0 - gate_sig))).astype(
        jnp.bfloat16
    )
    grad_up = (grad_product * swish).astype(jnp.bfloat16)
    grad_gate_w = contract_rows(normed_two, grad_gate)
    grad_up_w = contract_rows(normed_two, grad_up)
    grad_normed_two = times_transpose(grad_gate, full_gate) + times_transpose(grad_up, full_up)
    gain_two_grad = jnp.sum(grad_normed_two * hidden * scale_two, axis=0)
    scaled_two = grad_normed_two * gain_two
    grad_hidden = (
        upstream.astype(jnp.float32)
        + scale_two * scaled_two
        - hidden * scale_two**3 * jnp.mean(scaled_two * hidden, axis=-1, keepdims=True)
    )
    grad_hidden_low = grad_hidden.astype(jnp.bfloat16)
    grad_out_w = contract_rows(attended, grad_hidden_low)
    out_grad = to_groups(times_transpose(grad_hidden_low, full_out).astype(jnp.bfloat16))
    row_delta = jnp.sum(out_grad.astype(jnp.float32) * mixed_exact, axis=-1)

    def block_grads(key_block, source):
        weights_prob = probabilities(key_block, source)
        key_heads = key_block[0].reshape(sequences, local_len, KVH, HD)
        value_heads = key_block[1].reshape(sequences, local_len, KVH, HD)
        grad_weights = jnp.einsum(
            "sgrd,sugd->sgru", out_grad, value_heads, preferred_element_type=jnp.float32
        )
        grad_logits = (weights_prob * (grad_weights - row_delta[..., None])).astype(jnp.bfloat16)
        query_part = (
            jnp.einsum(
                "sgru,sugd->sgrd", grad_logits, key_heads, preferred_element_type=jnp.float32
            )
            * score_scale
        )
        key_part = (
            jnp.einsum("sgru,sgrd->sugd", grad_logits, queries, preferred_element_type=jnp.float32)
            * score_scale
        )
        value_part = jnp.einsum(
            "sgru,sgrd->sugd",
            weights_prob.astype(jnp.bfloat16),
            out_grad,
            preferred_element_type=jnp.float32,
        )
        return (
            query_part,
            jnp.stack(
                [
                    key_part.reshape(sequences, local_len, key_width),
                    value_part.reshape(sequences, local_len, key_width),
                ]
            ),
        )

    def add_pair(grad_query, grad_pair, key_block, source):
        query_part, pair_part = block_grads(key_block, source)
        return (grad_query + query_part, grad_pair + pair_part)

    def cycle_step(turn_index, running):
        grad_query, key_block, grad_pair = running
        source = (own_index - turn_index) % cycle_size
        grad_query, grad_pair = lax.cond(
            source <= own_index,
            lambda: add_pair(grad_query, grad_pair, key_block, source),
            lambda: (grad_query, grad_pair),
        )
        return (grad_query, move_block(key_block), move_grads(grad_pair))

    zero_pair = jnp.zeros((2, sequences, local_len, key_width), jnp.float32)
    grad_query, key_block, grad_pair = lax.fori_loop(
        0, cycle_size - 1, cycle_step, (zero_heads, own_block, zero_pair)
    )
    source = (own_index + 1) % cycle_size
    grad_query, grad_pair = lax.cond(
        source <= own_index,
        lambda: add_pair(grad_query, grad_pair, key_block, source),
        lambda: (grad_query, grad_pair),
    )
    grad_pair = move_grads(grad_pair)
    grad_q_rows = unrotate(
        to_rows(grad_query).reshape(sequences, local_len, HQ, HD), cos_table, sin_table
    ).reshape(token_rows, ATT)
    grad_k_rows = unrotate(
        grad_pair[0].reshape(sequences, local_len, KVH, HD), cos_table, sin_table
    ).reshape(token_rows, key_width)
    grad_v_rows = grad_pair[1].reshape(token_rows, key_width)
    grad_joined = jnp.concatenate([grad_q_rows, grad_k_rows, grad_v_rows], axis=-1).astype(
        jnp.bfloat16
    )
    grad_qkv_w = contract_rows(normed_one, grad_joined)
    grad_bias = jnp.sum(grad_joined.astype(jnp.float32), axis=0)
    grad_normed_one = times_transpose(grad_joined, full_qkv)
    gain_one_grad = jnp.sum(grad_normed_one * inputs * scale_one, axis=0)
    scaled_one = grad_normed_one * gain_one
    grad_input = (
        grad_hidden
        + scale_one * scaled_one
        - inputs * scale_one**3 * jnp.mean(scaled_one * inputs, axis=-1, keepdims=True)
    )
    halves = lax.axis_size("fsdp")
    group_size = lax.axis_size("dp") * lax.axis_size("ctx")
    per_core = (QKV + 2 * model_width) // halves
    packed_len = (per_core + group_size - 1) // group_size * group_size
    packed = jnp.concatenate(
        [
            grad_bias.reshape(halves, -1),
            gain_one_grad.reshape(halves, -1),
            gain_two_grad.reshape(halves, -1),
            jnp.zeros((halves, packed_len - per_core), jnp.float32),
        ],
        axis=1,
    )
    full_grads = (grad_qkv_w, grad_out_w, grad_gate_w, grad_up_w, grad_down, packed)
    partial_sums = (
        lax.psum_scatter(full_grads[0], ("dp", "ctx"), scatter_dimension=1, tiled=True),
        lax.psum_scatter(full_grads[1], ("dp", "ctx"), scatter_dimension=1, tiled=True),
        lax.psum_scatter(full_grads[2], ("dp", "ctx"), scatter_dimension=1, tiled=True),
        lax.psum_scatter(full_grads[3], ("dp", "ctx"), scatter_dimension=1, tiled=True),
        lax.psum_scatter(full_grads[4], ("dp", "ctx"), scatter_dimension=1, tiled=True),
        lax.psum_scatter(full_grads[5], ("dp", "ctx"), scatter_dimension=1, tiled=True),
    )
    partial_sums = (
        lax.psum_scatter(
            partial_sums[0].astype(jnp.bfloat16), "fsdp", scatter_dimension=0, tiled=True
        ).astype(jnp.float32),
        lax.psum_scatter(
            partial_sums[1].astype(jnp.bfloat16), "fsdp", scatter_dimension=0, tiled=True
        ).astype(jnp.float32),
        lax.psum_scatter(
            partial_sums[2].astype(jnp.bfloat16), "fsdp", scatter_dimension=0, tiled=True
        ).astype(jnp.float32),
        lax.psum_scatter(
            partial_sums[3].astype(jnp.bfloat16), "fsdp", scatter_dimension=0, tiled=True
        ).astype(jnp.float32),
        lax.psum_scatter(
            partial_sums[4].astype(jnp.bfloat16), "fsdp", scatter_dimension=0, tiled=True
        ).astype(jnp.float32),
        lax.psum_scatter(
            partial_sums[5].astype(jnp.bfloat16), "fsdp", scatter_dimension=0, tiled=True
        ).astype(jnp.float32),
    )
    own_pack = lax.all_gather(partial_sums[5], ("dp", "ctx"), axis=1, tiled=True)[0]
    bias_len = QKV // halves
    gain_len = model_width // halves
    return (
        activations.reshape(sequences, local_len, model_width),
        grad_input.reshape(sequences, local_len, model_width),
        partial_sums[0],
        own_pack[:bias_len],
        own_pack[bias_len : bias_len + gain_len],
        partial_sums[1],
        own_pack[bias_len + gain_len : bias_len + 2 * gain_len],
        partial_sums[2],
        partial_sums[3],
        partial_sums[4],
    )


def solution(mesh):
    in_specs = (
        P(("dp", "fsdp"), "ctx", None),
        P("fsdp", None),
        P("fsdp"),
        P("fsdp"),
        P("fsdp", None),
        P("fsdp"),
        P("fsdp", None),
        P("fsdp", None),
        P("fsdp", None),
        P(("dp", "fsdp"), "ctx", None),
    )
    out_specs = (
        P(("dp", "fsdp"), "ctx", None),
        P(("dp", "fsdp"), "ctx", None),
        P("fsdp", ("dp", "ctx")),
        P("fsdp"),
        P("fsdp"),
        P("fsdp", ("dp", "ctx")),
        P("fsdp"),
        P("fsdp", ("dp", "ctx")),
        P("fsdp", ("dp", "ctx")),
        P("fsdp", ("dp", "ctx")),
    )
    return jax.shard_map(
        per_device, mesh=mesh, in_specs=in_specs, out_specs=out_specs, check_vma=False
    )
```

profile of v0, /device:TPU:0, one launch (start us, length us, event | category | flops | bytes accessed | tf_op | source)
XLA Modules:
  0.0 1707.9 jit_solution(7177162886099779244)
XLA Ops:
  43.4 24.5 %conditional.6 = ((f32[1,2,3584]{2,1,0:T(2,128)}, f32[1,2,3584]{2,1,0:T(2,128)})) conditional(s32[]{:T(128)} %convert_element_type.185, (f32[1,2,3584]{2,1,0:T(2,128)}, f32[1,2,3584]{2,1,0:T(2,128)}) %tuple.64, (s32[]{:T(128)}, s32[3584]{0:T(1024)S(1)}, bf16[1,2,3584,64]{3,1,2,0:T(2,128)(2,1)S(1)}, bf16[2,1,512,128]{3,2,1,0:T(8,128)(2,1)S(1)}, ...), branch_computations={%region_1.2_spmd, %region_2.5_spmd} | conditional | flops 497302016 | bytes 39270524 | solution.py:153
  58.1 9.1 exponential_reduce_fusion
  71.0 38.0 %conditional.8 = (f32[1,2,3584,64]{2,3,1,0:T(8,128)}, f32[1,2,3584,64]{2,3,1,0:T(8,128)}) conditional(s32[]{:T(128)} %convert_element_type.185, f32[1,2,3584,64]{2,3,1,0:T(8,128)} %broadcast_in_dim.82, (s32[]{:T(128)}, s32[3584]{0:T(1024)S(1)}, bf16[1,2,3584,64]{3,1,2,0:T(2,128)(2,1)S(1)}, bf16[2,1,512,128]{3,2,1,0:T(8,128)(2,1)S(1)}, ...), branch_computations={%region_9.10_spmd, %region_10.11_spmd} | conditional | flops 3786539520 | bytes 105310368 | solution.py:153
  86.6 15.8 fusion.19
  108.9 13.0 conditional.9
  139.5 11.5 fusion.122
  150.9 11.3 fusion.123
  162.2 17.6 %multiply_convert_fusion.2 = (bf16[512,4864]{1,0:T(8,128)(2,1)}, bf16[512,4864]{1,0:T(8,128)(2,1)}, bf16[512,4864]{1,0:T(8,128)(2,1)}) fusion(f32[512,4864]{1,0:T(8,128)} %fusion.122, f32[512,4864]{1,0:T(8,128)} %fusion.123, bf16[4864,896]{1,0:T(8,128)(2,1)} %all-gather.14.cloned.1.call-done, bf16[1,512,896]{2,1,0:T(8,128)(2,1)} %param.31), kind=kOutput, calls=%fused_computation.98 | convolution fusion | flops 4500094976 | bytes 44498944 | tf_op jit(solution)/shard_map/dot_general | solution.py:63
  179.8 12.5 fusion.124
  223.5 43.6 %conditional.10 = ((f32[1,2,3584,64]{2,3,1,0:T(8,128)}, f32[2,1,512,128]{2,3,1,0:T(8,128)S(1)})) conditional(s32[]{:T(128)} %convert_element_type.185, (f32[1,2,3584,64]{2,3,1,0:T(8,128)}, f32[2,1,512,128]{2,3,1,0:T(8,128)S(1)}) %tuple.69, (s32[]{:T(128)}, s32[3584]{0:T(1024)S(1)}, bf16[1,2,3584,64]{3,1,2,0:T(2,128)(2,1)S(1)}, ...), branch_computations={%region_16.17_spmd, %region_17.18_spmd} | conditional | flops 2388591104 | bytes 97400960 | solution.py:278
  243.2 9.0 multiply_convert_fusion
  267.2 52.7 %collective-permute-start.1 = (bf16[2,1,512,128]{2,3,1,0:T(8,128)(2,1)S(1)}, bf16[2,1,512,128]{2,3,1,0:T(8,128)(2,1)S(1)}, u32[]{:S(2)}, u32[]{:S(2)}) collective-permute-start(bf16[2,1,512,128]{2,3,1,0:T(8,128)(2,1)S(1)} %convert_element_type.206), channel_id=1, source_target_pairs={{0,2},{2,0},{1,3},{3,1},{4,6},{6,4},{5,7},{7,5},{8,10},{10,8},{9,1... | collective-permute-start | bytes 786440 | tf_op jit(solution)/shard_map/while/body/eval_jaxpr/ppermute | solution.py:29
  319.8 15.7 collective-permute-done.1
  346.4 44.9 %collective-permute-start.2 = (bf16[2,1,512,128]{2,3,1,0:T(8,128)(2,1)S(1)}, bf16[2,1,512,128]{2,3,1,0:T(8,128)(2,1)S(1)}, u32[]{:S(2)}, u32[]{:S(2)}) collective-permute-start(bf16[2,1,512,128]{2,3,1,0:T(8,128)(2,1)S(1)} %convert_element_type.208), channel_id=1, source_target_pairs={{0,2},{2,0},{1,3},{3,1},{4,6},{6,4},{5,7},{7,5},{8,10},{10,8},{9,1... | collective-permute-start | bytes 786440 | tf_op jit(solution)/shard_map/ppermute | solution.py:29
  402.7 11.5 fusion.125
  414.2 11.4 fusion.126
  426.8 11.2 fusion.92
  440.0 96.8 %reduce-scatter.43.cloned.1.call-done = f32[896,72]{0,1:T(8,128)} async-done(((f32[896,1152]{0,1:T(8,128)}), f32[896,72]{0,1:T(8,128)}) %reduce-scatter.43.cloned.1.call-update) | async-done | bytes 258064
  538.9 359.1 %reduce-scatter.27.cloned.1.call-done = f32[896,304]{0,1:T(8,128)} async-done(((f32[896,4864]{0,1:T(8,128)}), f32[896,304]{0,1:T(8,128)}) %reduce-scatter.27.cloned.1.call-update) | async-done | bytes 1089552 | tf_op jit(solution)/shard_map/reduce_scatter | solution.py:333
  901.6 364.1 %reduce-scatter.29.cloned.1.call-done = f32[896,304]{0,1:T(8,128)} async-done(((f32[896,4864]{0,1:T(8,128)}), f32[896,304]{0,1:T(8,128)}) %reduce-scatter.29.cloned.1.call-update) | async-done | bytes 1089552 | tf_op jit(solution)/shard_map/reduce_scatter | solution.py:334
  1268.3 10.7 add_bitcast_fusion
  1284.7 82.8 %all-reduce.5 = bf16[2,1472]{1,0:T(2,128)(2,1)S(1)} all-reduce(f32[2,1472]{1,0:T(2,128)S(1)} %concatenate.62), channel_id=4, replica_groups=mesh['dp'=8,'ctx'=2,'fsdp'=2] {'dp','ctx'}, use_global_device_ids=true, to_apply=%region_26.27.clone | all-reduce | flops 2944 | bytes 17664
  1367.5 268.4 %reduce-scatter.31.cloned.1.call-done = f32[4864,56]{0,1:T(8,128)} async-done(((f32[4864,896]{0,1:T(8,128)}), f32[4864,56]{0,1:T(8,128)}) %reduce-scatter.31.cloned.1.call-update) | async-done | bytes 1089552 | tf_op jit(solution)/shard_map/reduce_scatter | solution.py:335
  1641.9 44.5 %all-reduce.3 = f32[1472]{0:T(1024)S(1)} all-reduce(f32[1472]{0:T(1024)S(1)} %fusion.111), channel_id=1, replica_groups=mesh['dp'=8,'ctx'=2,'fsdp'=2] {'dp','ctx'}, use_global_device_ids=true, to_apply=%add.3 | all-reduce | flops 1472 | bytes 11776
  (274 shorter events, 217.8 us)
Async XLA Ops:
  7.2 15.6 all-gather.6.cloned.1.call-start
  7.9 127.0 %all-gather.8.cloned.1.call-start = ((), (), s32[]{:S(2)}) async-start(), calls=%async_computation.11 | async-start | bytes 2408448 | tf_op jit(solution)/shard_map/all_gather | solution.py:87
  8.7 130.8 %all-gather.10.cloned.1.call-start = ((), (), s32[]{:S(2)}) async-start(), calls=%async_computation.12 | async-start | bytes 13074432 | tf_op jit(solution)/shard_map/all_gather | solution.py:89
  9.5 141.5 %all-gather.12.cloned.1.call-start = ((), (), s32[]{:S(2)}) async-start(), calls=%async_computation.13 | async-start | bytes 13074432 | tf_op jit(solution)/shard_map/all_gather | solution.py:90
  10.0 152.2 %all-gather.14.cloned.1.call-start = ((), (), s32[]{:S(2)}) async-start(), calls=%async_computation.14 | async-start | bytes 13074432 | tf_op jit(solution)/shard_map/all_gather | solution.py:91
  10.6 427.5 %reduce-scatter.45.cloned.1.call-start = ((), (), s32[]{:S(2)}) async-start(), calls=%async_computation.24 | async-start | bytes 3411968
  32.9 35.0 %collective-permute-start = (bf16[2,1,512,128]{3,2,1,0:T(8,128)(2,1)S(1)}, bf16[2,1,512,128]{3,2,1,0:T(8,128)(2,1)S(1)}, u32[]{:S(2)}, u32[]{:S(2)}) collective-permute-start(bf16[2,1,512,128]{3,2,1,0:T(8,128)(2,1)S(1)} %pad_maximum_fusion.3), channel_id=1, source_target_pairs={{0,2},{1,3},{4,6},{5,7},{8,10},{9,11},{12,14},{13,15},{16,18},{17,... | collective-permute-start | bytes 786440 | tf_op jit(solution)/shard_map/while/body/eval_jaxpr/ppermute | solution.py:23
  67.9 41.0 %copy-start.16 = (bf16[2,1,512,128]{3,2,1,0:T(8,128)(2,1)}, bf16[2,1,512,128]{3,2,1,0:T(8,128)(2,1)S(1)}, u32[]{:S(2)}) copy-start(bf16[2,1,512,128]{3,2,1,0:T(8,128)(2,1)S(1)} %collective-permute-done) | copy-start | bytes 786436
  205.3 331.5 %reduce-scatter.43.cloned.1.call-start = ((), (), s32[]{:S(2)}) async-start(), calls=%async_computation.23 | async-start | bytes 4386816
  267.2 68.4 %collective-permute-start.1 = (bf16[2,1,512,128]{2,3,1,0:T(8,128)(2,1)S(1)}, bf16[2,1,512,128]{2,3,1,0:T(8,128)(2,1)S(1)}, u32[]{:S(2)}, u32[]{:S(2)}) collective-permute-start(bf16[2,1,512,128]{2,3,1,0:T(8,128)(2,1)S(1)} %convert_element_type.206), channel_id=1, source_target_pairs={{0,2},{2,0},{1,3},{3,1},{4,6},{6,4},{5,7},{7,5},{8,10},{10,8},{9,1... | collective-permute-start | bytes 786440 | tf_op jit(solution)/shard_map/while/body/eval_jaxpr/ppermute | solution.py:29
  341.3 50.0 %copy-start.14 = (f32[512,64]{0,1:T(8,128)S(1)}, f32[512,64]{0,1:T(8,128)}, u32[]{:S(2)}) copy-start(f32[512,64]{0,1:T(8,128)} %copy-done.13) | copy-start | bytes 393220
  346.4 51.3 %collective-permute-start.2 = (bf16[2,1,512,128]{2,3,1,0:T(8,128)(2,1)S(1)}, bf16[2,1,512,128]{2,3,1,0:T(8,128)(2,1)S(1)}, u32[]{:S(2)}, u32[]{:S(2)}) collective-permute-start(bf16[2,1,512,128]{2,3,1,0:T(8,128)(2,1)S(1)} %convert_element_type.208), channel_id=1, source_target_pairs={{0,2},{2,0},{1,3},{3,1},{4,6},{6,4},{5,7},{7,5},{8,10},{10,8},{9,1... | collective-permute-start | bytes 786440 | tf_op jit(solution)/shard_map/ppermute | solution.py:29
  401.5 496.4 %reduce-scatter.27.cloned.1.call-start = ((), (), s32[]{:S(2)}) async-start(), calls=%async_computation.15 | async-start | bytes 18522112 | tf_op jit(solution)/shard_map/reduce_scatter | solution.py:333
  414.2 851.5 %reduce-scatter.29.cloned.1.call-start = ((), (), s32[]{:S(2)}) async-start(), calls=%async_computation.16 | async-start | bytes 18522112 | tf_op jit(solution)/shard_map/reduce_scatter | solution.py:334
  425.7 1210.2 %reduce-scatter.31.cloned.1.call-start = ((), (), s32[]{:S(2)}) async-start(), calls=%async_computation.17 | async-start | bytes 18522112 | tf_op jit(solution)/shard_map/reduce_scatter | solution.py:335
  438.0 1252.9 %reduce-scatter.35.cloned.1.call-start = ((), (), s32[]{:S(2)}) async-start(), calls=%async_computation.19 | async-start | bytes 344064
  439.9 1252.7 %reduce-scatter.33.cloned.1.call-start = ((), (), s32[]{:S(2)}) async-start(), calls=%async_computation.18 | async-start | bytes 344064
  538.6 729.7 %copy-start.5 = (f32[512,896]{1,0:T(8,128)S(1)}, f32[512,896]{1,0:T(8,128)}, u32[]{:S(2)}) copy-start(f32[512,896]{1,0:T(8,128)} %copy-done.3) | copy-start | bytes 5505028
  538.6 1155.7 %reduce-scatter.37.cloned.1.call-start = ((), (), s32[]{:S(2)}) async-start(), calls=%async_computation.20 | async-start | bytes 1032192
  900.4 795.9 %reduce-scatter.39.cloned.1.call-start = ((), (), s32[]{:S(2)}) async-start(), calls=%async_computation.21 | async-start | bytes 1032192
  1268.2 430.7 %reduce-scatter.41.cloned.1.call-start = ((), (), s32[]{:S(2)}) async-start(), calls=%async_computation.22 | async-start | bytes 1867776
  1284.5 403.2 %copy-start.2 = (f32[512,896]{1,0:T(8,128)S(1)}, f32[512,896]{1,0:T(8,128)}, u32[]{:S(2)}) copy-start(f32[512,896]{1,0:T(8,128)} %copy-done.1) | copy-start | bytes 5505028
  1284.5 403.2 %copy-start.9 = (bf16[1,512,896]{2,1,0:T(8,128)(2,1)S(1)}, bf16[1,512,896]{2,1,0:T(8,128)(2,1)}, u32[]{:S(2)}) copy-start(bf16[1,512,896]{2,1,0:T(8,128)(2,1)} %param.22) | copy-start | bytes 2752516
  1284.5 403.2 %copy-start.41 = (f32[512]{0:T(512)S(1)}, f32[512]{0:T(512)}, u32[]{:S(2)}) copy-start(f32[512]{0:T(512)} %get-tuple-element.453) | copy-start | bytes 6148
  (40 other events, 295.0 us)
Sparse Core Ops, SparseCore 0:
  9.6 13.2 all-gather.5
  24.4 11.0 all-gather.7
  37.0 22.1 all-gather.9
  60.6 22.1 all-gather.11
  84.2 22.1 all-gather.13
  205.4 140.1 reduce-scatter.44
  401.6 135.0 reduce-scatter.42
  539.1 358.8 reduce-scatter.26
  900.4 365.2 reduce-scatter.28
  1267.9 367.9 reduce-scatter.30
  1638.8 13.2 reduce-scatter.34
  1654.8 8.7 reduce-scatter.32
  1666.0 9.2 reduce-scatter.36
  1677.5 9.2 reduce-scatter.38
  1689.0 9.8 reduce-scatter.40
where the time goes:
time: 1710 us
  waiting for transfers between devices  1120 us (65%)
  matrix products  196 us (11%)
  blocking collectives  132 us (8%)
  starting transfers between devices  102 us (6%)
  local copies, waits for them, and re-layouts  81.9 us (5%)
  other arithmetic  49.3 us (3%)
  between operations  17.5 us (1%)
    reduce_scatter x1, waiting for transfers between devices, per_device(): lax.psum_scatter(full_grads[3], ('dp', 'ctx'), scatter_dimension=1, tiled...  364 us
    reduce_scatter x1, waiting for transfers between devices, per_device(): lax.psum_scatter(full_grads[2], ('dp', 'ctx'), scatter_dimension=1, tiled...  359 us
    reduce_scatter x1, waiting for transfers between devices, per_device(): lax.psum_scatter(full_grads[4], ('dp', 'ctx'), scatter_dimension=1, tiled...  268 us
    unnamed x4, blocking collectives  132 us
    unnamed x22, waiting for transfers between devices  101 us
    ppermute x2, starting transfers between devices, shifted_2(): return lax.ppermute(value, axis, pairs)  97.6 us
    dot_general x5, matrix products, times_transpose(): lax.dot_general(left, right, (((1,), (1,)), ((), ())), preferred_element_...  47.6 us
    dot_general x5, matrix products, contract_rows(): lax.dot_general(left, right, (((0,), (0,)), ((), ())), preferred_element_...  40.6 us
  transfers between devices with their start and end apart: 18, of which 8 were waited for; matrix products, arithmetic and copies ran while one was open for 16% of the time, Pallas kernels for 0%

commit v1 on v0

v1 whole, which is shorter than its diff:
```python
import functools

import jax
import jax.numpy as jnp
from jax import lax
from jax.experimental import pallas as pl
from jax.experimental.pallas import tpu as pltpu
from jax.sharding import PartitionSpec as P

HQ = 14
KVH = 2
HD = 64
ATT = 896
QKV = 1152
GROUP = 7

epsilon = 1e-06
rope_base = 1000000.0
masked_score = -1e30
f32 = jnp.float32
bf16 = jnp.bfloat16


def dot_rows(left, right):
    return lax.dot_general(left, right, (((0,), (0,)), ((), ())), preferred_element_type=f32)


def dot_last(left, right):
    return lax.dot_general(left, right, (((1,), (1,)), ((), ())), preferred_element_type=f32)


def dot(left, right):
    return jnp.dot(left, right, preferred_element_type=f32)


def partner(value, axis, bit):
    return lax.ppermute(value, axis, [(i, i ^ (1 << bit)) for i in range(lax.axis_size(axis))])


def bits_of(axis):
    return lax.axis_size(axis).bit_length() - 1


class Halving:
    def __init__(self, blocks, order):
        self.inner = blocks.shape[1:]
        self.dp_bits = bits_of("dp")
        self.bits = self.dp_bits + bits_of("ctx")
        self.order = list(order)
        self.free = self.held = blocks.reshape((2,) * self.bits + self.inner)

    def step(self):
        if not self.order:
            return
        axis, bit = self.order.pop(0)
        dim = (self.dp_bits if axis == "dp" else self.bits) - 1 - bit
        mine = (lax.axis_index(axis) >> bit) & 1
        sent = lax.dynamic_slice_in_dim(self.free, 1 - mine, 1, dim)
        kept = lax.dynamic_slice_in_dim(self.held, mine, 1, dim)
        self.free = (kept.astype(f32) + partner(sent, axis, bit).astype(f32)).astype(bf16)
        self.held = self.free

    def finish(self):
        while self.order:
            self.step()
        return self.free.reshape(self.inner)


def after(arrays, sums):
    together = lax.optimization_barrier((tuple(arrays), tuple(one.held for one in sums)))
    for one, held in zip(sums, together[1]):
        one.held = held
    return together[0]


def step_all(sums):
    for one in sums:
        one.step()


def sum_everywhere(vector):
    for axis in ("fsdp", "ctx", "dp"):
        for bit in range(bits_of(axis)):
            vector = vector + partner(vector, axis, bit)
    return vector


def tables(positions, width):
    frequency = rope_base ** (-(2.0 * jnp.arange(HD // 2, dtype=f32)) / HD)
    angles = positions[:, None] * frequency[None, :]
    cos_table = jnp.tile(jnp.cos(angles), (1, width // (HD // 2)))
    sin_table = jnp.tile(jnp.sin(angles), (1, width // (HD // 2)))
    return cos_table, sin_table


def swap_halves(flat):
    half = HD // 2
    lower = (jnp.arange(flat.shape[1]) % HD < half)[None, :]
    return jnp.where(lower, -jnp.roll(flat, -half, axis=1), jnp.roll(flat, half, axis=1))


def head_cols(ref, index):
    return ref[:, index * HD : (index + 1) * HD]


def visible_mask(tile, length, ctx_len):
    first = lax.axis_index("ctx") * ctx_len + pl.program_id(0) * tile
    rows = first + lax.broadcasted_iota(jnp.int32, (tile, length), 0)
    return lax.broadcasted_iota(jnp.int32, (tile, length), 1) <= rows


def attend_kernel(ctx_len, q_ref, k_ref, v_ref, o_ref, lse_ref):
    tile, length = q_ref.shape[0], k_ref.shape[0]
    mask = visible_mask(tile, length, ctx_len)
    outs, logs = [], []
    for head in range(HQ):
        group = head // GROUP
        scores = dot_last(head_cols(q_ref, head), head_cols(k_ref, group))
        scores = jnp.where(mask, scores, masked_score)
        top = jnp.max(scores, axis=-1, keepdims=True)
        exps = jnp.exp(scores - top)
        total = jnp.sum(exps, axis=-1, keepdims=True)
        probs = (exps * (1.0 / total)).astype(bf16)
        outs.append(dot(probs, head_cols(v_ref, group)))
        logs.append(top + jnp.log(total))
    o_ref[...] = jnp.concatenate(outs, axis=1).astype(bf16)
    lse_ref[...] = jnp.concatenate(logs + [jnp.zeros((tile, 128 - HQ), f32)], axis=1)


def attend_grad_kernel(ctx_len, q_ref, do_ref, lse_ref, k_ref, v_ref, dq_ref, dk_ref, dv_ref):
    tile, length = q_ref.shape[0], k_ref.shape[0]
    mask = visible_mask(tile, length, ctx_len)

    @pl.when(pl.program_id(0) == 0)
    def _():
        dk_ref[...] = jnp.zeros_like(dk_ref)
        dv_ref[...] = jnp.zeros_like(dv_ref)

    parts = []
    for group in range(KVH):
        keys, values = head_cols(k_ref, group), head_cols(v_ref, group)
        dk = jnp.zeros((HD, length), f32)
        dv = jnp.zeros((HD, length), f32)
        for head in range(group * GROUP, (group + 1) * GROUP):
            query, grad = head_cols(q_ref, head), head_cols(do_ref, head)
            scores = dot_last(query, keys) - lse_ref[:, head : head + 1]
            probs = jnp.exp(jnp.where(mask, scores, masked_score))
            grad_probs = dot_last(grad, values)
            delta = jnp.sum(probs * grad_probs, axis=-1, keepdims=True)
            grad_scores = (probs * (grad_probs - delta)).astype(bf16)
            parts.append(dot(grad_scores, keys) * HD ** (-0.5))
            dk += dot_rows(query, grad_scores)
            dv += dot_rows(grad, probs.astype(bf16))
        dk_ref[group * HD : (group + 1) * HD, :] += dk
        dv_ref[group * HD : (group + 1) * HD, :] += dv
    dq_ref[...] = jnp.concatenate(parts, axis=1)


def rows_spec(tile, width):
    return pl.BlockSpec((tile, width), lambda step: (step, 0))


def whole_spec(rows, width):
    return pl.BlockSpec((rows, width), lambda step: (0, 0))


def attend(queries, keys, values):
    rows, length = queries.shape[0], keys.shape[0]
    tile = min(256, rows)
    return pl.pallas_call(
        functools.partial(attend_kernel, rows),
        grid=(rows // tile,),
        in_specs=[rows_spec(tile, ATT), whole_spec(length, KVH * HD), whole_spec(length, KVH * HD)],
        out_specs=[rows_spec(tile, ATT), rows_spec(tile, 128)],
        out_shape=[
            jax.ShapeDtypeStruct((rows, ATT), bf16),
            jax.ShapeDtypeStruct((rows, 128), f32),
        ],
        compiler_params=pltpu.CompilerParams(vmem_limit_bytes=40 << 20),
        cost_estimate=pl.CostEstimate(
            flops=8 * rows * length * ATT, bytes_accessed=4 << 20, transcendentals=rows * length * HQ
        ),
    )(queries, keys, values)


def attend_grad(queries, grads, lse, keys, values):
    rows, length = queries.shape[0], keys.shape[0]
    tile = min(256, rows)
    pair = whole_spec(length, KVH * HD)
    flipped = whole_spec(KVH * HD, length)
    return pl.pallas_call(
        functools.partial(attend_grad_kernel, rows),
        grid=(rows // tile,),
        in_specs=[rows_spec(tile, ATT), rows_spec(tile, ATT), rows_spec(tile, 128), pair, pair],
        out_specs=[rows_spec(tile, ATT), flipped, flipped],
        out_shape=[
            jax.ShapeDtypeStruct((rows, ATT), f32),
            jax.ShapeDtypeStruct((KVH * HD, length), f32),
            jax.ShapeDtypeStruct((KVH * HD, length), f32),
        ],
        compiler_params=pltpu.CompilerParams(vmem_limit_bytes=40 << 20),
        cost_estimate=pl.CostEstimate(
            flops=24 * rows * length * ATT, bytes_accessed=6 << 20, transcendentals=rows * length * HQ
        ),
    )(queries, grads, lse, keys, values)


def per_device(layer_input, w_qkv, b_qkv, g_attn, w_out, g_mlp, w_gate, w_up, w_down, cotangent):
    sequences, local_len, width = layer_input.shape
    token_rows = sequences * local_len
    half = width // 2
    key_width = KVH * HD
    ctx_size, dp_size = lax.axis_size("ctx"), lax.axis_size("dp")
    group_size = ctx_size * dp_size
    own_index = lax.axis_index("ctx")
    first = lax.axis_index("fsdp") == 0

    def swap(value):
        return partner(value, "fsdp", 0)

    def joined_rows(own, other):
        axis = 0
        return jnp.where(
            first,
            jnp.concatenate([own, other], axis=axis),
            jnp.concatenate([other, own], axis=axis),
        )

    def joined_cols(own, other):
        return jnp.where(
            first, jnp.concatenate([own, other], axis=1), jnp.concatenate([other, own], axis=1)
        )

    def split_cols(value):
        cut = value.shape[1] // 2
        left, right = value[:, :cut], value[:, cut:]
        return jnp.where(first, left, right), jnp.where(first, right, left)

    vector = jnp.concatenate([b_qkv, g_attn, g_mlp])
    full_qkv = joined_rows(w_qkv, swap(w_qkv))
    vector_other = swap(vector)
    full_out = joined_rows(w_out, swap(w_out))
    gate_other, up_other, down_other = swap(w_gate), swap(w_up), swap(w_down)
    bias_len = b_qkv.shape[0]
    full_bias = joined_rows(vector[:bias_len], vector_other[:bias_len]).astype(f32)
    gain_one = joined_rows(
        vector[bias_len : bias_len + half], vector_other[bias_len : bias_len + half]
    ).astype(f32)
    gain_two = joined_rows(vector[bias_len + half :], vector_other[bias_len + half :]).astype(f32)

    inputs = layer_input.reshape(token_rows, width).astype(f32)
    scale_one = lax.rsqrt(jnp.mean(inputs * inputs, axis=-1, keepdims=True) + epsilon)
    normed_one = (inputs * scale_one * gain_one).astype(bf16)
    joined = dot(normed_one, full_qkv) + full_bias
    positions = (own_index * local_len + jnp.arange(local_len, dtype=jnp.int32)).astype(f32)
    cos_table, sin_table = tables(positions, ATT + key_width)
    cos_table = jnp.tile(cos_table, (sequences, 1))
    sin_table = jnp.tile(sin_table, (sequences, 1))
    turned = joined[:, : ATT + key_width]
    turned = (turned * cos_table + swap_halves(turned) * sin_table).astype(bf16)
    queries = (turned[:, :ATT] * HD ** (-0.5)).astype(bf16).reshape(sequences, local_len, ATT)
    own_pair = jnp.concatenate([turned[:, ATT:], joined[:, ATT + key_width :].astype(bf16)], axis=1)
    own_pair = own_pair.reshape(sequences, local_len, 2 * key_width)
    if ctx_size == 2:
        other_pair = partner(own_pair, "ctx", 0)
        pairs = jnp.where(
            own_index == 0,
            jnp.concatenate([own_pair, other_pair], axis=1),
            jnp.concatenate([other_pair, own_pair], axis=1),
        )
    else:
        pairs = lax.all_gather(own_pair, "ctx", axis=1, tiled=True)
    keys, values = pairs[..., :key_width], pairs[..., key_width:]
    mixed = [attend(queries[s], keys[s], values[s]) for s in range(sequences)]
    attended = jnp.concatenate([m[0] for m in mixed], axis=0)
    hidden = inputs + dot(attended, full_out)
    scale_two = lax.rsqrt(jnp.mean(hidden * hidden, axis=-1, keepdims=True) + epsilon)
    normed_two = (hidden * scale_two * gain_two).astype(bf16)
    two_mine, two_other = split_cols(normed_two)
    gate_pre = dot(two_mine, w_gate) + dot(two_other, gate_other)
    up_value = dot(two_mine, w_up) + dot(two_other, up_other)
    gate_sig = jax.nn.sigmoid(gate_pre)
    swish = gate_pre * gate_sig
    product = (swish * up_value).astype(bf16)
    product_mine, product_other = split_cols(product)
    upstream = cotangent.reshape(token_rows, width)

    ctx_order = [("ctx", bit) for bit in range(bits_of("ctx"))]
    near = [("dp", 0)] if dp_size > 1 else []
    far = [("dp", bit) for bit in range(1, bits_of("dp"))]
    order_a = ctx_order + near + far
    order_b = near + ctx_order + far

    down_sent = swap(dot_rows(upstream, product_other).astype(bf16))
    down_sum = (dot_rows(upstream, product_mine) + down_sent.astype(f32)).astype(bf16)
    down_sum = down_sum.reshape(group_size, width // group_size, -1)
    cut = (down_sum.shape[2] // 256) * 128
    downs = [Halving(down_sum[..., :cut], order_a), Halving(down_sum[..., cut:], order_b)]

    product_grads = after(
        (dot_last(upstream, w_down), dot_last(upstream, down_other), product_mine, product_other),
        downs,
    )
    step_all(downs)
    grad_product = joined_cols(product_grads[0], product_grads[1])
    activations = hidden + (dot(product_grads[2], w_down) + dot(product_grads[3], down_other))
    grad_gate = (grad_product * up_value * gate_sig * (1.0 + gate_pre * (1.0 - gate_sig))).astype(
        bf16
    )
    grad_up = (grad_product * swish).astype(bf16)

    def weight_sums(grad):
        sent = swap(dot_rows(grad, two_other).astype(bf16))
        total = (dot_rows(grad, two_mine) + sent.astype(f32)).astype(bf16)
        total = total.reshape(group_size, -1, half)
        cut = total.shape[1] // 16 * 8
        return [Halving(total[:, :cut], order_a), Halving(total[:, cut:], order_b)]

    gates, ups = weight_sums(grad_gate), weight_sums(grad_up)
    grad_gate, grad_up = after((grad_gate, grad_up), downs + gates + ups)
    step_all(downs + gates)

    grad_normed_two = joined_cols(
        dot_last(grad_gate, w_gate) + dot_last(grad_up, w_up),
        dot_last(grad_gate, gate_other) + dot_last(grad_up, up_other),
    )
    gain_two_grad = jnp.sum(grad_normed_two * hidden * scale_two, axis=0)
    scaled_two = grad_normed_two * gain_two
    grad_hidden = (
        upstream.astype(f32)
        + scale_two * scaled_two
        - hidden * scale_two**3 * jnp.mean(scaled_two * hidden, axis=-1, keepdims=True)
    )
    grad_hidden, grad_hidden_low = after((grad_hidden, grad_hidden.astype(bf16)), downs + gates)
    step_all(downs + gates + ups)
    out_grad = dot_last(grad_hidden_low, full_out).astype(bf16).reshape(sequences, local_len, ATT)
    grads = [
        attend_grad(queries[s], out_grad[s], mixed[s][1], keys[s], values[s])
        for s in range(sequences)
    ]
    grad_q = jnp.concatenate([g[0] for g in grads], axis=0)
    grad_pairs = jnp.stack([jnp.concatenate([g[1], g[2]], axis=0).T for g in grads])
    grad_q, grad_pairs = after((grad_q, grad_pairs), downs + gates + ups)
    grad_down = jnp.concatenate([one.finish() for one in downs], axis=1).astype(f32).T
    grad_gate_w = jnp.concatenate([one.finish() for one in gates], axis=0).astype(f32).T
    grad_up_w = jnp.concatenate([one.finish() for one in ups], axis=0).astype(f32).T
    if ctx_size == 2:
        lower, upper = grad_pairs[:, :local_len], grad_pairs[:, local_len:]
        sent = jnp.where(own_index == 0, upper, lower).astype(bf16)
        grad_pair = jnp.where(own_index == 0, lower, upper) + partner(sent, "ctx", 0).astype(f32)
    else:
        grad_pair = lax.psum_scatter(
            grad_pairs.astype(bf16), "ctx", scatter_dimension=1, tiled=True
        ).astype(f32)
    grad_pair = grad_pair.reshape(token_rows, 2 * key_width)
    grad_turned = jnp.concatenate([grad_q, grad_pair[:, :key_width]], axis=1)
    grad_turned = grad_turned * cos_table - swap_halves(grad_turned * sin_table)
    grad_joined = jnp.concatenate([grad_turned, grad_pair[:, key_width:]], axis=1).astype(bf16)

    att_mine, att_other = split_cols(attended)
    one_mine, one_other = split_cols(normed_one)

    def by_group(qkv_part, out_part):
        return jnp.concatenate(
            [
                qkv_part.reshape(group_size, -1, half),
                out_part.reshape(group_size, -1, half),
            ],
            axis=1,
        )

    small_sent = swap(
        by_group(dot_rows(grad_joined, one_other), dot_rows(grad_hidden_low, att_other)).astype(bf16)
    )
    small = by_group(dot_rows(grad_joined, one_mine), dot_rows(grad_hidden_low, att_mine))
    small = (small + small_sent.astype(f32)).astype(bf16)
    small = Halving(small, order_a).finish().astype(f32)
    qkv_rows = QKV // group_size
    grad_qkv_w, grad_out_w = small[:qkv_rows].T, small[qkv_rows:].T

    grad_bias = jnp.sum(grad_joined.astype(f32), axis=0)
    grad_normed_one = dot_last(grad_joined, full_qkv)
    gain_one_grad = jnp.sum(grad_normed_one * inputs * scale_one, axis=0)
    scaled_one = grad_normed_one * gain_one
    grad_input = (
        grad_hidden
        + scale_one * scaled_one
        - inputs * scale_one**3 * jnp.mean(scaled_one * inputs, axis=-1, keepdims=True)
    )
    packed = sum_everywhere(jnp.concatenate([grad_bias, gain_one_grad, gain_two_grad])[None])[0]

    def own_half(begin, length):
        part = packed[begin : begin + length]
        return jnp.where(first, part[: length // 2], part[length // 2 :])

    return (
        activations.reshape(sequences, local_len, width),
        grad_input.reshape(sequences, local_len, width),
        grad_qkv_w,
        own_half(0, QKV),
        own_half(QKV, width),
        grad_out_w,
        own_half(QKV + width, width),
        grad_gate_w,
        grad_up_w,
        grad_down,
    )


def solution(mesh):
    in_specs = (
        P(("dp", "fsdp"), "ctx", None),
        P("fsdp", None),
        P("fsdp"),
        P("fsdp"),
        P("fsdp", None),
        P("fsdp"),
        P("fsdp", None),
        P("fsdp", None),
        P("fsdp", None),
        P(("dp", "fsdp"), "ctx", None),
    )
    out_specs = (
        P(("dp", "fsdp"), "ctx", None),
        P(("dp", "fsdp"), "ctx", None),
        P("fsdp", ("dp", "ctx")),
        P("fsdp"),
        P("fsdp"),
        P("fsdp", ("dp", "ctx")),
        P("fsdp"),
        P("fsdp", ("dp", "ctx")),
        P("fsdp", ("dp", "ctx")),
        P("fsdp", ("dp", "ctx")),
    )
    return jax.shard_map(
        per_device, mesh=mesh, in_specs=in_specs, out_specs=out_specs, check_vma=False
    )
```

time: 1710 us -> 448 us (0.26)
  waiting for transfers between devices: 1120 us -> 75.4 us
  blocking collectives: 132 us -> 0 us
  matrix products: 196 us -> 123 us
  starting transfers between devices: 102 us -> 47 us
  Pallas kernels: 0 us -> 44.7 us
    reduce_scatter x3 -> x0, waiting for transfers between devices: 992 us -> none  [the longest x1 364 us: per_device(): lax.psum_scatter(full_grads[3], ('dp', 'ctx'), scatter_dimension=1, tiled...]
    unnamed x4 -> x0, blocking collectives: 132 us -> none
    unnamed x22 -> x0, waiting for transfers between devices: 101 us -> none
    dot_general x24 -> x26, matrix products: 196 us -> 123 us  [the longest x8 43.5 us: dot(): return jnp.dot(left, right, preferred_element_type=f32)]
    ppermute x3 -> x45, waiting for transfers between devices: 20.5 us -> 75.4 us  [partner(): lax.ppermute(value, axis, [(i, i ^ 1 << bit) for i in range(lax.axis_size...]
    ppermute x3 -> x45, starting transfers between devices: 101 us -> 47 us  [partner(): lax.ppermute(value, axis, [(i, i ^ 1 << bit) for i in range(lax.axis_size...]
    pallas_call x0 -> x2, Pallas kernels: none -> 44.7 us  [the longest x1 25.8 us: attend_grad(): pl.pallas_call(functools.partial(attend_grad_kernel, rows), grid=(rows //...]
    convert_element_type x20 -> x33, other arithmetic: 14.4 us -> 41.1 us  [the longest x21 18.9 us: step(): (kept.astype(f32) + partner(sent, axis, bit).astype(f32)).astype(bf16)]
  transfers between devices with their start and end apart: 18 -> 45, of which waited for: 8 -> 13; matrix products, arithmetic and copies ran while one was open for 16% -> 53% of each run, Pallas kernels for 0% -> 10%
where the time goes in v1:
time: 448 us; the launch traced here: 441 us
  matrix products  123 us (27%)
  local copies, waits for them, and re-layouts  84.5 us (19%)
  waiting for transfers between devices  75.4 us (17%)
  other arithmetic  64.1 us (14%)
  starting transfers between devices  47 us (10%)
  Pallas kernels  44.7 us (10%)
    ppermute x45, waiting for transfers between devices, partner(): lax.ppermute(value, axis, [(i, i ^ 1 << bit) for i in range(lax.axis_size...  75.4 us
    ppermute x45, starting transfers between devices, partner(): lax.ppermute(value, axis, [(i, i ^ 1 << bit) for i in range(lax.axis_size...  47 us
    dot_general x8, matrix products, dot(): return jnp.dot(left, right, preferred_element_type=f32)  43.5 us
    dot_general x10, matrix products, dot_rows(): lax.dot_general(left, right, (((0,), (0,)), ((), ())), preferred_element_...  41 us
    dot_general x8, matrix products, dot_last(): lax.dot_general(left, right, (((1,), (1,)), ((), ())), preferred_element_...  38.7 us
    pallas_call x1, Pallas kernels, attend_grad(): pl.pallas_call(functools.partial(attend_grad_kernel, rows), grid=(rows //...  25.8 us
    convert_element_type x21, other arithmetic, step(): (kept.astype(f32) + partner(sent, axis, bit).astype(f32)).astype(bf16)  18.9 us
    pallas_call x1, Pallas kernels, attend(): pl.pallas_call(functools.partial(attend_kernel, rows), grid=(rows // tile...  18.9 us
  transfers between devices with their start and end apart: 45, of which 13 were waited for; matrix products, arithmetic and copies ran while one was open for 53% of the time, Pallas kernels for 10%

profile of v1, /device:TPU:0, one launch (start us, length us, event | category | flops | bytes accessed | tf_op | source)
XLA Modules:
  0.0 441.4 jit_solution(6949427358851422612)
XLA Ops:
  26.0 6.4 %collective-permute-done.2 = bf16[1,512,256]{2,1,0:T(8,128)(2,1)S(1)} collective-permute-done((bf16[1,512,256]{2,1,0:T(8,128)(2,1)S(1)}, bf16[1,512,256]{2,1,0:T(8,128)(2,1)S(1)}, u32[]{:S(2)}, u32[]{:S(2)}) %collective-permute-start.2) | collective-permute-done | bytes 262176 | tf_op jit(solution)/shard_map/ppermute | solution.py:37
  32.8 18.9 %shard_map.177 = (bf16[512,896]{1,0:T(8,128)(2,1)S(1)}, f32[512,128]{1,0:T(8,128)S(1)}) custom-call(bf16[512,896]{1,0:T(8,128)(2,1)S(1)} %slice_multiply_fusion.1.q_ref, bf16[1024,128]{1,0:T(8,128)(2,1)S(1)} %get-tuple-element.123.k_ref, bf16[1024,128]{1,0:T(8,128)(2,1)S(1)} %get-tuple-element.122.v_ref), custom_call_target="tpu_custom_call" | custom-call | flops 3758096384 | bytes 4194304 | tf_op jit(solution)/shard_map/pallas_call | solution.py:170
  59.3 5.3 %fusion.74 = f32[512,4864]{1,0:T(8,128)} fusion(bf16[512,448]{1,0:T(8,128)(2,1)S(1)} %get-tuple-element.121, bf16[448,4864]{1,0:T(8,128)(2,1)S(1)} %bitcast.147), kind=kOutput, calls=%fused_computation.211 | convolution fusion | flops 2231369728 | bytes 14778368 | tf_op jit(solution)/shard_map/dot_general | solution.py:33
  69.7 11.2 %multiply_convert_fusion.2 = (bf16[512,4864]{1,0:T(8,128)(2,1)}, f32[512,4864]{1,0:T(8,128)}) fusion(f32[512,4864]{1,0:T(8,128)S(1)} %convolution_add_fusion.1, f32[512,4864]{1,0:T(8,128)} %fusion.74, bf16[512,448]{1,0:T(8,128)(2,1)S(1)} %get-tuple-element.120, bf16[448,4864]{1,0:T(8,128)(2,1)} %collective-permute-done.6), kind=kOutput, calls=%fused_computation.3 | convolution fusion | flops 2248802304 | bytes 39682048 | tf_op jit(solution)/shard_map/dot_general | solution.py:33
  92.6 6.9 %fusion.23 = f32[512,2432]{1,0:T(8,128)} fusion(bf16[2432,896]{1,0:T(8,128)(2,1)} %collective-permute-done.4, bf16[1,512,896]{2,1,0:T(8,128)(2,1)S(1)} %copy-done.55), kind=kOutput, calls=%fused_computation.82 | convolution fusion | flops 2231369728 | bytes 10256384 | tf_op jit(solution)/shard_map/dot_general | solution.py:29
  105.3 14.6 %multiply_convert_fusion = (bf16[512,4864]{1,0:T(8,128)(2,1)}, bf16[512,4864]{1,0:T(8,128)(2,1)S(1)}) fusion(f32[512,2432]{1,0:T(8,128)} %fusion.25, f32[512,2432]{1,0:T(8,128)} %fusion.23, pred[]{:T(512)S(6)} %eq.11, f32[512,4864]{1,0:T(8,128)S(1)} %convolution_add_fusion.1, f32[512,4864]{1,0:T(8,128)} %get-tuple-element.137), kind=kLoop, calls=%fused_computation.1 | loop fusion | flops 39845888 | bytes 39845888 | tf_op jit(solution)/shard_map/convert_element_type | solution.py:310
  127.7 7.1 %convolution_convert_fusion = bf16[4864,448]{0,1:T(8,128)(2,1)} fusion(bf16[512,4864]{1,0:T(8,128)(2,1)} %get-tuple-element.51, bf16[512,448]{1,0:T(8,128)(2,1)S(1)} %get-tuple-element.120), kind=kOutput, calls=%fused_computation.12 | convolution fusion | flops 2233548800 | bytes 9797632 | tf_op jit(solution)/shard_map/dot_general | solution.py:25
  135.0 5.2 %fusion.75 = f32[512,896]{1,0:T(8,128)S(1)} fusion(bf16[512,2432]{1,0:T(8,128)(2,1)S(1)} %copy-done.35, bf16[2432,896]{1,0:T(8,128)(2,1)} %param.18), kind=kOutput, calls=%fused_computation.212 | convolution fusion | flops 2231369728 | bytes 8683520 | tf_op jit(solution)/shard_map/dot_general | solution.py:33
  141.9 6.8 %add_bitcast_fusion = f32[1,512,896]{2,1,0:T(8,128)} fusion(f32[512,896]{1,0:T(8,128)S(1)} %get-tuple-element.135, f32[512,896]{1,0:T(8,128)S(1)} %fusion.75, bf16[512,2432]{1,0:T(8,128)(2,1)S(1)} %copy-done.33, bf16[2432,896]{1,0:T(8,128)(2,1)} %collective-permute-done.4), kind=kOutput, calls=%fused_computation.62 | convolution fusion | flops 2232287232 | bytes 12353536 | tf_op jit(solution)/shard_map/dot_general | solution.py:33
  154.1 14.4 %collective-permute-done.9 = bf16[2,2,1,2,56,1280]{5,4,3,2,1,0:T(8,128)(2,1)S(1)} collective-permute-done((bf16[2,2,1,2,56,1280]{5,4,3,2,1,0:T(8,128)(2,1)S(1)}, bf16[2,2,1,2,56,1280]{5,4,3,2,1,0:T(8,128)(2,1)S(1)}, u32[]{:S(2)}, u32[]{:S(2)}) %collective-permute-start.9) | collective-permute-done | bytes 1146912 | tf_op jit(solution)/shard_map/ppermute | solution.py:37
  171.0 7.3 %add_convert_fusion.1 = bf16[4864,448]{0,1:T(8,128)(2,1)} fusion(bf16[4864,448]{0,1:T(8,128)(2,1)} %collective-permute-done.10, bf16[512,4864]{1,0:T(8,128)(2,1)S(1)} %bitcast.140, bf16[512,448]{1,0:T(8,128)(2,1)S(1)} %get-tuple-element.121), kind=kOutput, calls=%fused_computation.9 | convolution fusion | flops 2237906944 | bytes 14155776 | tf_op jit(solution)/shard_map/dot_general | solution.py:25
  178.3 7.3 %copy.75 = bf16[4864,448]{1,0:T(8,128)(2,1)} copy(bf16[4864,448]{0,1:T(8,128)(2,1)} %add_convert_fusion.1) | data formatting | bytes 8716288 | tf_op jit(solution)/shard_map/convert_element_type | solution.py:314
  190.7 8.3 %add_convert_fusion = bf16[4864,448]{0,1:T(8,128)(2,1)} fusion(bf16[4864,448]{0,1:T(8,128)(2,1)} %collective-permute-done.11, bf16[512,4864]{1,0:T(8,128)(2,1)} %get-tuple-element.51, bf16[512,448]{1,0:T(8,128)(2,1)S(1)} %get-tuple-element.121), kind=kOutput, calls=%fused_computation.8 | convolution fusion | flops 2237906944 | bytes 14155776 | tf_op jit(solution)/shard_map/dot_general | solution.py:25
  199.0 7.3 %copy.76 = bf16[4864,448]{1,0:T(8,128)(2,1)} copy(bf16[4864,448]{0,1:T(8,128)(2,1)} %add_convert_fusion) | data formatting | bytes 8716288 | tf_op jit(solution)/shard_map/convert_element_type | solution.py:314
  206.3 5.2 %fusion.66 = (bf16[16,152,448]{2,1,0:T(8,128)(2,1)}, bf16[16,152,448]{2,1,0:T(8,128)(2,1)}) fusion(bf16[16,304,448]{2,1,0:T(8,128)(2,1)} %bitcast.123), kind=kLoop, calls=%fused_computation.203 | loop fusion | bytes 8716288 | tf_op jit(solution)/shard_map/slice | solution.py:317
  211.5 6.3 %fusion.76 = f32[512,448]{0,1:T(8,128)S(1)} fusion(bf16[512,4864]{1,0:T(8,128)(2,1)} %get-tuple-element.51, bf16[448,4864]{1,0:T(8,128)(2,1)} %param.17), kind=kOutput, calls=%fused_computation.213 | convolution fusion | flops 2231369728 | bytes 10256384 | tf_op jit(solution)/shard_map/dot_general | solution.py:29
  225.9 5.6 %convolution_add_fusion.3 = f32[512,448]{0,1:T(8,128)} fusion(f32[512,448]{0,1:T(8,128)S(1)} %fusion.77, bf16[512,4864]{1,0:T(8,128)(2,1)S(1)} %bitcast.142, bf16[448,4864]{1,0:T(8,128)(2,1)} %collective-permute-done.5), kind=kOutput, calls=%fused_computation.69 | convolution fusion | flops 2231599104 | bytes 11173888 | tf_op jit(solution)/shard_map/dot_general | solution.py:29
  253.4 14.0 %collective-permute-done.14 = bf16[2,2,2,1,152,448]{5,4,3,2,1,0:T(8,128)(2,1)S(1)} collective-permute-done((bf16[2,2,2,1,152,448]{5,4,3,2,1,0:T(8,128)(2,1)S(1)}, bf16[2,2,2,1,152,448]{5,4,3,2,1,0:T(8,128)(2,1)S(1)}, u32[]{:S(2)}, u32[]{:S(2)}) %collective-permute-start.14) | collective-permute-done | bytes 1089568 | tf_op jit(solution)/shard_map/ppermute | solution.py:37
  274.8 25.8 %shard_map.178 = (f32[512,896]{1,0:T(8,128)S(1)}, f32[128,1024]{1,0:T(8,128)S(1)}, f32[128,1024]{1,0:T(8,128)S(1)}) custom-call(bf16[512,896]{1,0:T(8,128)(2,1)S(1)} %copy-done.1, bf16[512,896]{1,0:T(8,128)(2,1)S(1)} %convolution_convert_fusion.4.do_ref, f32[512,128]{1,0:T(8,128)S(1)} %get-tuple-element.58.lse_ref, bf16[1024,128]{1,0:T(8,128)(2,1)S(1)} %copy-done.5, ...), custom_call_target="tpu_custom_call" | custom-call | flops 11274289152 | bytes 6291456 | tf_op jit(solution)/shard_map/pallas_call | solution.py:191
  331.7 6.3 %collective-permute-done.40 = bf16[2,2,1,1,152,448]{5,4,3,2,1,0:T(8,128)(2,1)S(1)} collective-permute-done((bf16[2,2,1,1,152,448]{5,4,3,2,1,0:T(8,128)(2,1)S(1)}, bf16[2,2,1,1,152,448]{5,4,3,2,1,0:T(8,128)(2,1)S(1)}, u32[]{:S(2)}, u32[]{:S(2)}) %collective-permute-start.40) | collective-permute-done | bytes 544800 | tf_op jit(solution)/shard_map/ppermute | solution.py:37
  398.8 5.2 %collective-permute-done.32 = f32[1,2944]{1,0:T(1,128)S(1)} collective-permute-done((f32[1,2944]{1,0:T(1,128)S(1)}, f32[1,2944]{1,0:T(1,128)S(1)}, u32[]{:S(2)}, u32[]{:S(2)}) %collective-permute-start.32) | collective-permute-done | bytes 11808 | tf_op jit(solution)/shard_map/ppermute | solution.py:37
  406.9 8.1 %collective-permute-done.24 = bf16[2,2,2,1,128,448]{4,5,3,2,1,0:T(8,128)(2,1)} collective-permute-done((bf16[2,2,2,1,128,448]{4,5,3,2,1,0:T(8,128)(2,1)}, bf16[2,2,2,1,128,448]{4,5,3,2,1,0:T(8,128)(2,1)}, u32[]{:S(2)}, u32[]{:S(2)}) %collective-permute-start.24) | collective-permute-done | bytes 917536 | tf_op jit(solution)/shard_map/ppermute | solution.py:37
  427.1 5.9 %collective-permute-done.26 = bf16[2,1,1,1,128,448]{4,5,3,2,1,0:T(8,128)(2,1)S(1)} collective-permute-done((bf16[2,1,1,1,128,448]{4,5,3,2,1,0:T(8,128)(2,1)S(1)}, bf16[2,1,1,1,128,448]{4,5,3,2,1,0:T(8,128)(2,1)S(1)}, u32[]{:S(2)}, u32[]{:S(2)}) %collective-permute-start.26) | collective-permute-done | bytes 229408 | tf_op jit(solution)/shard_map/ppermute | solution.py:37
  434.3 5.2 %collective-permute-done.27 = bf16[1,1,1,1,128,448]{4,5,3,2,1,0:T(8,128)(2,1)S(1)} collective-permute-done((bf16[1,1,1,1,128,448]{4,5,3,2,1,0:T(8,128)(2,1)S(1)}, bf16[1,1,1,1,128,448]{4,5,3,2,1,0:T(8,128)(2,1)S(1)}, u32[]{:S(2)}, u32[]{:S(2)}) %collective-permute-start.27) | collective-permute-done | bytes 114720 | tf_op jit(solution)/shard_map/ppermute | solution.py:37
  (427 shorter events, 224.3 us)
Async XLA Ops:
  3.3 48.4 %collective-permute-start.3 = (bf16[448,896]{1,0:T(8,128)(2,1)}, bf16[448,896]{1,0:T(8,128)(2,1)}, u32[]{:S(2)}, u32[]{:S(2)}) collective-permute-start(bf16[448,896]{1,0:T(8,128)(2,1)} %param.14), channel_id=1, source_target_pairs={{0,1},{1,0},{2,3},{3,2},{4,5},{5,4},{6,7},{7,6},{8,9},{9,8},{10,11... | collective-permute-start | bytes 2408456 | tf_op jit(solution)/shard_map/ppermute | solution.py:37
  3.7 88.9 %collective-permute-start.4 = (bf16[2432,896]{1,0:T(8,128)(2,1)}, bf16[2432,896]{1,0:T(8,128)(2,1)}, u32[]{:S(2)}, u32[]{:S(2)}) collective-permute-start(bf16[2432,896]{1,0:T(8,128)(2,1)} %param.18), channel_id=1, source_target_pairs={{0,1},{1,0},{2,3},{3,2},{4,5},{5,4},{6,7},{7,6},{8,9},{9,8},{10,11... | collective-permute-start | bytes 13074440 | tf_op jit(solution)/shard_map/ppermute | solution.py:37
  3.8 60.8 %collective-permute-start.5 = (bf16[448,4864]{1,0:T(8,128)(2,1)}, bf16[448,4864]{1,0:T(8,128)(2,1)}, u32[]{:S(2)}, u32[]{:S(2)}) collective-permute-start(bf16[448,4864]{1,0:T(8,128)(2,1)} %param.16), channel_id=1, source_target_pairs={{0,1},{1,0},{2,3},{3,2},{4,5},{5,4},{6,7},{7,6},{8,9},{9,8},{10,11... | collective-permute-start | bytes 13074440 | tf_op jit(solution)/shard_map/ppermute | solution.py:37
  14.9 54.8 %collective-permute-start.6 = (bf16[448,4864]{1,0:T(8,128)(2,1)}, bf16[448,4864]{1,0:T(8,128)(2,1)}, u32[]{:S(2)}, u32[]{:S(2)}) collective-permute-start(bf16[448,4864]{1,0:T(8,128)(2,1)} %param.17), channel_id=1, source_target_pairs={{0,1},{1,0},{2,3},{3,2},{4,5},{5,4},{6,7},{7,6},{8,9},{9,8},{10,11... | collective-permute-start | bytes 13074440 | tf_op jit(solution)/shard_map/ppermute | solution.py:37
  124.5 46.4 %collective-permute-start.10 = (bf16[4864,448]{0,1:T(8,128)(2,1)}, bf16[4864,448]{0,1:T(8,128)(2,1)}, u32[]{:S(2)}, u32[]{:S(2)}) collective-permute-start(bf16[4864,448]{0,1:T(8,128)(2,1)} %convolution_convert_fusion.1), channel_id=1, source_target_pairs={{0,1},{1,0},{2,3},{3,2},{4,5},{5,4},{6,7},{7,6},{8,9},{9,8},{10,11... | collective-permute-start | bytes 13074440 | tf_op jit(solution)/shard_map/ppermute | solution.py:37
  125.9 25.3 %collective-permute-start.8 = (bf16[2,2,2,1,56,1152]{5,4,3,2,1,0:T(8,128)(2,1)S(1)}, bf16[2,2,2,1,56,1152]{5,4,3,2,1,0:T(8,128)(2,1)S(1)}, u32[]{:S(2)}, u32[]{:S(2)}) collective-permute-start(bf16[2,2,2,1,56,1152]{5,4,3,2,1,0:T(8,128)(2,1)S(1)} %constant_dynamic-slice_fusion.28), channel_id=1, source_target_pairs={{0,2},{2,0},{1,3},{3,1},{4,6},{6,4},{5,7},{7,5},{8,10},{10,8},{9,1... | collective-permute-start | bytes 3096584 | tf_op jit(solution)/shard_map/ppermute | solution.py:37
  134.8 55.9 %collective-permute-start.11 = (bf16[4864,448]{0,1:T(8,128)(2,1)}, bf16[4864,448]{0,1:T(8,128)(2,1)}, u32[]{:S(2)}, u32[]{:S(2)}) collective-permute-start(bf16[4864,448]{0,1:T(8,128)(2,1)} %convolution_convert_fusion), channel_id=1, source_target_pairs={{0,1},{1,0},{2,3},{3,2},{4,5},{5,4},{6,7},{7,6},{8,9},{9,8},{10,11... | collective-permute-start | bytes 13074440 | tf_op jit(solution)/shard_map/ppermute | solution.py:37
  140.4 28.2 %collective-permute-start.9 = (bf16[2,2,1,2,56,1280]{5,4,3,2,1,0:T(8,128)(2,1)S(1)}, bf16[2,2,1,2,56,1280]{5,4,3,2,1,0:T(8,128)(2,1)S(1)}, u32[]{:S(2)}, u32[]{:S(2)}) collective-permute-start(bf16[2,2,1,2,56,1280]{5,4,3,2,1,0:T(8,128)(2,1)S(1)} %constant_dynamic-slice_fusion.27), channel_id=1, source_target_pairs={{0,4},{4,0},{8,12},{12,8},{16,20},{20,16},{24,28},{28,24},{1,5},{5... | collective-permute-start | bytes 3440648 | tf_op jit(solution)/shard_map/ppermute | solution.py:37
  152.3 88.2 %collective-permute-start.12 = (bf16[2,2,1,1,56,1152]{5,4,3,2,1,0:T(8,128)(2,1)}, bf16[2,2,1,1,56,1152]{5,4,3,2,1,0:T(8,128)(2,1)}, u32[]{:S(2)}, u32[]{:S(2)}) collective-permute-start(bf16[2,2,1,1,56,1152]{5,4,3,2,1,0:T(8,128)(2,1)} %constant_dynamic-slice_fusion.26), channel_id=1, source_target_pairs={{0,4},{4,0},{8,12},{12,8},{16,20},{20,16},{24,28},{28,24},{1,5},{5... | collective-permute-start | bytes 1548296 | tf_op jit(solution)/shard_map/ppermute | solution.py:37
  170.6 74.8 %collective-permute-start.13 = (bf16[2,2,1,1,56,1280]{5,4,3,2,1,0:T(8,128)(2,1)}, bf16[2,2,1,1,56,1280]{5,4,3,2,1,0:T(8,128)(2,1)}, u32[]{:S(2)}, u32[]{:S(2)}) collective-permute-start(bf16[2,2,1,1,56,1280]{5,4,3,2,1,0:T(8,128)(2,1)} %constant_dynamic-slice_fusion.25), channel_id=1, source_target_pairs={{0,2},{2,0},{1,3},{3,1},{4,6},{6,4},{5,7},{7,5},{8,10},{10,8},{9,1... | collective-permute-start | bytes 1720328 | tf_op jit(solution)/shard_map/ppermute | solution.py:37
  237.1 30.4 %collective-permute-start.14 = (bf16[2,2,2,1,152,448]{5,4,3,2,1,0:T(8,128)(2,1)S(1)}, bf16[2,2,2,1,152,448]{5,4,3,2,1,0:T(8,128)(2,1)S(1)}, u32[]{:S(2)}, u32[]{:S(2)}) collective-permute-start(bf16[2,2,2,1,152,448]{5,4,3,2,1,0:T(8,128)(2,1)S(1)} %constant_dynamic-slice_fusion.24), channel_id=1, source_target_pairs={{0,2},{2,0},{1,3},{3,1},{4,6},{6,4},{5,7},{7,5},{8,10},{10,8},{9,1... | collective-permute-start | bytes 3268616 | tf_op jit(solution)/shard_map/ppermute | solution.py:37
  239.0 31.6 %collective-permute-start.15 = (bf16[2,2,1,2,152,448]{5,4,3,2,1,0:T(8,128)(2,1)S(1)}, bf16[2,2,1,2,152,448]{5,4,3,2,1,0:T(8,128)(2,1)S(1)}, u32[]{:S(2)}, u32[]{:S(2)}) collective-permute-start(bf16[2,2,1,2,152,448]{5,4,3,2,1,0:T(8,128)(2,1)S(1)} %constant_dynamic-slice_fusion.23), channel_id=1, source_target_pairs={{0,4},{4,0},{8,12},{12,8},{16,20},{20,16},{24,28},{28,24},{1,5},{5... | collective-permute-start | bytes 3268616 | tf_op jit(solution)/shard_map/ppermute | solution.py:37
  242.6 77.5 %collective-permute-start.16 = (bf16[2,1,1,1,56,1152]{5,4,3,2,1,0:T(8,128)(2,1)S(1)}, bf16[2,1,1,1,56,1152]{5,4,3,2,1,0:T(8,128)(2,1)}, u32[]{:S(2)}, u32[]{:S(2)}) collective-permute-start(bf16[2,1,1,1,56,1152]{5,4,3,2,1,0:T(8,128)(2,1)S(1)} %constant_dynamic-slice_fusion.22), channel_id=1, source_target_pairs={{0,8},{4,12},{8,0},{12,4},{16,24},{20,28},{24,16},{28,20},{1,9},{5... | collective-permute-start | bytes 774152 | tf_op jit(solution)/shard_map/ppermute | solution.py:37
  247.5 69.9 %collective-permute-start.17 = (bf16[2,1,1,1,56,1280]{5,4,3,2,1,0:T(8,128)(2,1)}, bf16[2,1,1,1,56,1280]{5,4,3,2,1,0:T(8,128)(2,1)}, u32[]{:S(2)}, u32[]{:S(2)}) collective-permute-start(bf16[2,1,1,1,56,1280]{5,4,3,2,1,0:T(8,128)(2,1)} %constant_dynamic-slice_fusion.21), channel_id=1, source_target_pairs={{0,8},{4,12},{8,0},{12,4},{16,24},{20,28},{24,16},{28,20},{1,9},{5... | collective-permute-start | bytes 860168 | tf_op jit(solution)/shard_map/ppermute | solution.py:37
  247.9 67.1 %collective-permute-start.20 = (bf16[2,2,2,1,152,448]{5,4,3,2,1,0:T(8,128)(2,1)}, bf16[2,2,2,1,152,448]{5,4,3,2,1,0:T(8,128)(2,1)}, u32[]{:S(2)}, u32[]{:S(2)}) collective-permute-start(bf16[2,2,2,1,152,448]{5,4,3,2,1,0:T(8,128)(2,1)} %constant_dynamic-slice_fusion.18), channel_id=1, source_target_pairs={{0,2},{2,0},{1,3},{3,1},{4,6},{6,4},{5,7},{7,5},{8,10},{10,8},{9,1... | collective-permute-start | bytes 3268616 | tf_op jit(solution)/shard_map/ppermute | solution.py:37
  267.5 43.7 %collective-permute-start.21 = (bf16[2,2,1,2,152,448]{5,4,3,2,1,0:T(8,128)(2,1)}, bf16[2,2,1,2,152,448]{5,4,3,2,1,0:T(8,128)(2,1)}, u32[]{:S(2)}, u32[]{:S(2)}) collective-permute-start(bf16[2,2,1,2,152,448]{5,4,3,2,1,0:T(8,128)(2,1)} %constant_dynamic-slice_fusion.17), channel_id=1, source_target_pairs={{0,4},{4,0},{8,12},{12,8},{16,20},{20,16},{24,28},{28,24},{1,5},{5... | collective-permute-start | bytes 3268616 | tf_op jit(solution)/shard_map/ppermute | solution.py:37
  338.0 29.6 %collective-permute-start.35 = (bf16[2,1,1,1,152,448]{5,4,3,2,1,0:T(8,128)(2,1)}, bf16[2,1,1,1,152,448]{5,4,3,2,1,0:T(8,128)(2,1)S(1)}, u32[]{:S(2)}, u32[]{:S(2)}) collective-permute-start(bf16[2,1,1,1,152,448]{5,4,3,2,1,0:T(8,128)(2,1)} %constant_dynamic-slice_fusion.9), channel_id=1, source_target_pairs={{0,8},{4,12},{8,0},{12,4},{16,24},{20,28},{24,16},{28,20},{1,9},{5... | collective-permute-start | bytes 817160 | tf_op jit(solution)/shard_map/ppermute | solution.py:37
  340.7 29.2 %collective-permute-start.33 = (bf16[2,1,1,1,152,448]{5,4,3,2,1,0:T(8,128)(2,1)}, bf16[2,1,1,1,152,448]{5,4,3,2,1,0:T(8,128)(2,1)}, u32[]{:S(2)}, u32[]{:S(2)}) collective-permute-start(bf16[2,1,1,1,152,448]{5,4,3,2,1,0:T(8,128)(2,1)} %constant_dynamic-slice_fusion.11), channel_id=1, source_target_pairs={{0,8},{4,12},{8,0},{12,4},{16,24},{20,28},{24,16},{28,20},{1,9},{5... | collective-permute-start | bytes 817160 | tf_op jit(solution)/shard_map/ppermute | solution.py:37
  341.1 33.6 %collective-permute-start.41 = (bf16[2,1,1,1,152,448]{5,4,3,2,1,0:T(8,128)(2,1)}, bf16[2,1,1,1,152,448]{5,4,3,2,1,0:T(8,128)(2,1)}, u32[]{:S(2)}, u32[]{:S(2)}) collective-permute-start(bf16[2,1,1,1,152,448]{5,4,3,2,1,0:T(8,128)(2,1)} %constant_dynamic-slice_fusion.3), channel_id=1, source_target_pairs={{0,8},{4,12},{8,0},{12,4},{16,24},{20,28},{24,16},{28,20},{1,9},{5... | collective-permute-start | bytes 817160 | tf_op jit(solution)/shard_map/ppermute | solution.py:37
  343.8 51.2 %collective-permute-start.38 = (bf16[2,1,1,1,152,448]{5,4,3,2,1,0:T(8,128)(2,1)}, bf16[2,1,1,1,152,448]{5,4,3,2,1,0:T(8,128)(2,1)}, u32[]{:S(2)}, u32[]{:S(2)}) collective-permute-start(bf16[2,1,1,1,152,448]{5,4,3,2,1,0:T(8,128)(2,1)} %constant_dynamic-slice_fusion.6), channel_id=1, source_target_pairs={{0,8},{4,12},{8,0},{12,4},{16,24},{20,28},{24,16},{28,20},{1,9},{5... | collective-permute-start | bytes 817160 | tf_op jit(solution)/shard_map/ppermute | solution.py:37
  360.9 24.0 %collective-permute-start.23 = (bf16[16,128,448]{1,2,0:T(8,128)(2,1)}, bf16[16,128,448]{1,2,0:T(8,128)(2,1)S(1)}, u32[]{:S(2)}, u32[]{:S(2)}) collective-permute-start(bf16[16,128,448]{1,2,0:T(8,128)(2,1)} %copy.89), channel_id=1, source_target_pairs={{0,1},{1,0},{2,3},{3,2},{4,5},{5,4},{6,7},{7,6},{8,9},{9,8},{10,11... | collective-permute-start | bytes 5505032 | tf_op jit(solution)/shard_map/ppermute | solution.py:37
  369.9 35.4 %collective-permute-start.36 = (bf16[1,1,1,1,152,448]{5,4,3,2,1,0:T(8,128)(2,1)S(1)}, bf16[1,1,1,1,152,448]{5,4,3,2,1,0:T(8,128)(2,1)}, u32[]{:S(2)}, u32[]{:S(2)}) collective-permute-start(bf16[1,1,1,1,152,448]{5,4,3,2,1,0:T(8,128)(2,1)S(1)} %constant_dynamic-slice_fusion.8), channel_id=1, source_target_pairs={{0,16},{4,20},{8,24},{12,28},{16,0},{20,4},{24,8},{28,12},{1,17},{... | collective-permute-start | bytes 408584 | tf_op jit(solution)/shard_map/ppermute | solution.py:37
  374.5 43.7 %collective-permute-start.34 = (bf16[1,1,1,1,152,448]{5,4,3,2,1,0:T(8,128)(2,1)}, bf16[1,1,1,1,152,448]{5,4,3,2,1,0:T(8,128)(2,1)}, u32[]{:S(2)}, u32[]{:S(2)}) collective-permute-start(bf16[1,1,1,1,152,448]{5,4,3,2,1,0:T(8,128)(2,1)} %constant_dynamic-slice_fusion.10), channel_id=1, source_target_pairs={{0,16},{4,20},{8,24},{12,28},{16,0},{20,4},{24,8},{28,12},{1,17},{... | collective-permute-start | bytes 408584 | tf_op jit(solution)/shard_map/ppermute | solution.py:37
  382.2 37.8 %collective-permute-start.42 = (bf16[1,1,1,1,152,448]{5,4,3,2,1,0:T(8,128)(2,1)}, bf16[1,1,1,1,152,448]{5,4,3,2,1,0:T(8,128)(2,1)}, u32[]{:S(2)}, u32[]{:S(2)}) collective-permute-start(bf16[1,1,1,1,152,448]{5,4,3,2,1,0:T(8,128)(2,1)} %constant_dynamic-slice_fusion.2), channel_id=1, source_target_pairs={{0,16},{4,20},{8,24},{12,28},{16,0},{20,4},{24,8},{28,12},{1,17},{... | collective-permute-start | bytes 408584 | tf_op jit(solution)/shard_map/ppermute | solution.py:37
  (116 other events, 946.7 us)
